TPU v7x, 32 devices: a whole 2x2x4 slice. The times are simulated.
32 devices in a mesh: batch: 8 (over z, core), ctx: 4 (over y, x).
Axes of the slice: x: 2, y: 2, z: 4, core: 2. Of those that a mesh axis runs over, the one named last changes fastest.
Arguments:
- tokens: bfloat16 [8, 512, 2048], P('batch', 'ctx'), may hold values from -6 to 6
- out_grad: bfloat16 [8, 512, 2048], P('batch', 'ctx'), may hold values from -6 to 6
- ln1_gain: bfloat16 [2048], P(('batch', 'ctx')), may hold values from 0.5 to 1.5
- ln1_shift: bfloat16 [2048], P(('batch', 'ctx')), may hold values from -3 to 3
- qkv_weight: bfloat16 [2048, 6144], P(('batch', 'ctx')), may hold values from -0.125 to 0.125
- qkv_bias: bfloat16 [6144], P(('batch', 'ctx')), may hold values from -3 to 3
- out_weight: bfloat16 [2048, 2048], P(('batch', 'ctx')), may hold values from -1 to 1
- ln2_gain: bfloat16 [2048], P(('batch', 'ctx')), may hold values from 0.5 to 1.5
- ln2_shift: bfloat16 [2048], P(('batch', 'ctx')), may hold values from -3 to 3
- gate_weight: bfloat16 [2048, 5632], P(('batch', 'ctx')), may hold values from -0.125 to 0.125
- up_weight: bfloat16 [2048, 5632], P(('batch', 'ctx')), may hold values from -0.125 to 0.125
- down_weight: bfloat16 [2048, 5632], P(('batch', 'ctx')), may hold values from -0.078125 to 0.078125
Outputs:
- mixed: bfloat16 [8, 512, 2048], P('batch', 'ctx')
- tokens_grad: float32 [8, 512, 2048], P('batch', 'ctx')
- ln1_gain_grad: float32 [2048], P(('batch', 'ctx'))
- ln1_shift_grad: float32 [2048], P(('batch', 'ctx'))
- qkv_weight_grad: float32 [2048, 6144], P(('batch', 'ctx'))
- qkv_bias_grad: float32 [6144], P(('batch', 'ctx'))
- out_weight_grad: float32 [2048, 2048], P(('batch', 'ctx'))
- ln2_gain_grad: float32 [2048], P(('batch', 'ctx'))
- ln2_shift_grad: float32 [2048], P(('batch', 'ctx'))
- gate_weight_grad: float32 [2048, 5632], P(('batch', 'ctx'))
- up_weight_grad: float32 [2048, 5632], P(('batch', 'ctx'))
- down_weight_grad: float32 [2048, 5632], P(('batch', 'ctx'))
All inputs are finite; a program needn't handle non-finite values.
Results may differ from a plain program's by a relative error of at most 0.03.
Values may be sent and summed in bfloat16 or wider, within the bound.
A program may use at most 576 MiB of HBM per device.

v0:
```python
import jax
import jax.numpy as jnp
from jax import lax
from jax.sharding import PartitionSpec as P

D = 2048
FF = 5632
H = 32
HD = 64
ROT = 16


def layer_norm(values, gain, shift):
    centre = jnp.mean(values, axis=-1, keepdims=True)
    centred = values - centre
    spread = jnp.mean(centred * centred, axis=-1, keepdims=True)
    return centred * lax.rsqrt(spread + 1e-05) * gain + shift


def rotary(values, positions):
    half_dims = ROT // 2
    frequency = 10000.0 ** (-jnp.arange(half_dims, dtype=jnp.float32) * 2.0 / ROT)
    angles = positions.astype(jnp.float32)[:, None] * frequency[None, :]
    cosine_term = jnp.cos(angles)[:, None, :]
    sine_term = jnp.sin(angles)[:, None, :]
    first_half = values[..., :half_dims]
    second_half = values[..., half_dims:ROT]
    return jnp.concatenate(
        [
            first_half * cosine_term - second_half * sine_term,
            second_half * cosine_term + first_half * sine_term,
            values[..., ROT:],
        ],
        axis=-1,
    )


def swish_product(gate_value, up_value):
    return gate_value / (1.0 + jnp.exp(-gate_value)) * up_value


def project_back(left, right):
    return lax.dot_general(
        left, right, (((1,), (1,)), ((), ())), preferred_element_type=jnp.float32
    )


def outer_rows(left, right):
    return lax.dot_general(
        left, right, (((0,), (0,)), ((), ())), preferred_element_type=jnp.float32
    )


def local(
    tokens,
    out_grad,
    ln1_gain,
    ln1_shift,
    qkv_weight,
    qkv_bias,
    out_weight,
    ln2_gain,
    ln2_shift,
    gate_weight,
    up_weight,
    down_weight,
):
    local_rows = tokens.shape[1]
    seq_length = local_rows * lax.axis_size("ctx")
    inputs = tokens.reshape(local_rows, D).astype(jnp.float32)
    cotangent = out_grad.reshape(local_rows, D).astype(jnp.float32)
    places = lax.axis_index("ctx") * local_rows + jnp.arange(local_rows, dtype=jnp.int32)
    attn_set = (
        lax.all_gather(qkv_weight, ("batch", "ctx"), axis=0, tiled=True),
        lax.all_gather(out_weight, ("batch", "ctx"), axis=0, tiled=True),
        lax.all_gather(qkv_bias, ("batch", "ctx"), axis=0, tiled=True),
        lax.all_gather(ln1_gain, ("batch", "ctx"), axis=0, tiled=True),
        lax.all_gather(ln1_shift, ("batch", "ctx"), axis=0, tiled=True),
    )
    gain_one = attn_set[3].astype(jnp.float32)
    shift_one = attn_set[4].astype(jnp.float32)
    normed = layer_norm(inputs, gain_one, shift_one)
    normed_low = normed.astype(jnp.bfloat16)
    projected = jnp.dot(normed_low, attn_set[0], preferred_element_type=jnp.float32) + attn_set[
        2
    ].astype(jnp.float32)
    pair_heads = projected[:, : 2 * D].reshape(local_rows, 2 * H, HD)
    turned = rotary(pair_heads, places)
    queries = turned[:, :H].astype(jnp.bfloat16)
    key_rows = turned[:, H:].reshape(local_rows, D).astype(jnp.bfloat16)
    value_rows = projected[:, 2 * D :].astype(jnp.bfloat16)
    start_state = (
        jnp.full((H, local_rows), -1e30, jnp.float32),
        jnp.zeros((H, local_rows), jnp.float32),
        jnp.zeros((H, local_rows, HD), jnp.float32),
    )
    carry = start_state
    key_piece = lax.all_gather(key_rows, "ctx", axis=0, tiled=True)
    value_piece = lax.all_gather(value_rows, "ctx", axis=0, tiled=True)
    piece_rows = key_piece.shape[0]
    block_rows = 512
    block_count = piece_rows // block_rows

    def inner(state, block):
        largest, totals, accum = state
        key_block, value_block, offset = block
        raw_scores = (
            jnp.einsum("qhd,khd->hqk", queries, key_block, preferred_element_type=jnp.float32)
            * 0.125
        )
        key_places = offset + jnp.arange(block_rows, dtype=jnp.int32)
        allowed = (key_places[None, :] <= places[:, None])[None]
        raw_scores = jnp.where(allowed, raw_scores, -1e30)
        new_largest = jnp.maximum(largest, jnp.max(raw_scores, axis=-1))
        weights = jnp.where(allowed, jnp.exp(raw_scores - new_largest[..., None]), 0.0)
        factor = jnp.exp(largest - new_largest)
        totals = totals * factor + jnp.sum(weights, axis=-1)
        accum = accum * factor[..., None] + jnp.einsum(
            "hqk,khd->hqd",
            weights.astype(jnp.bfloat16),
            value_block,
            preferred_element_type=jnp.float32,
        )
        return ((new_largest, totals, accum), None)

    offsets = jnp.arange(block_count, dtype=jnp.int32) * block_rows
    blocks = (
        key_piece.reshape(block_count, block_rows, H, HD),
        value_piece.reshape(block_count, block_rows, H, HD),
        offsets,
    )
    carry, unused = lax.scan(inner, carry, blocks)
    largest, totals, accum = carry
    attended = jnp.transpose(accum / totals[..., None], (1, 0, 2)).reshape(local_rows, D)
    log_total = largest + jnp.log(totals)
    attended_low = attended.astype(jnp.bfloat16)
    middle = inputs + jnp.dot(attended_low, attn_set[1], preferred_element_type=jnp.float32)
    mlp_set = (
        lax.all_gather(gate_weight, ("batch", "ctx"), axis=0, tiled=True),
        lax.all_gather(up_weight, ("batch", "ctx"), axis=0, tiled=True),
        lax.all_gather(down_weight, ("batch", "ctx"), axis=0, tiled=True),
        lax.all_gather(ln2_gain, ("batch", "ctx"), axis=0, tiled=True),
        lax.all_gather(ln2_shift, ("batch", "ctx"), axis=0, tiled=True),
    )
    gain_two = mlp_set[3].astype(jnp.float32)
    shift_two = mlp_set[4].astype(jnp.float32)
    normed_two_low = layer_norm(middle, gain_two, shift_two).astype(jnp.bfloat16)
    gate_value = jnp.dot(normed_two_low, mlp_set[0], preferred_element_type=jnp.float32)
    up_value = jnp.dot(normed_two_low, mlp_set[1], preferred_element_type=jnp.float32)
    hidden_low = swish_product(gate_value, up_value).astype(jnp.bfloat16)
    mixed = (middle + project_back(hidden_low, mlp_set[2])).astype(jnp.bfloat16)
    mlp_back = (
        lax.all_gather(gate_weight, ("batch", "ctx"), axis=0, tiled=True),
        lax.all_gather(up_weight, ("batch", "ctx"), axis=0, tiled=True),
        lax.all_gather(down_weight, ("batch", "ctx"), axis=0, tiled=True),
        lax.all_gather(ln2_gain, ("batch", "ctx"), axis=0, tiled=True),
        lax.all_gather(ln2_shift, ("batch", "ctx"), axis=0, tiled=True),
    )
    attn_back = (
        lax.all_gather(qkv_weight, ("batch", "ctx"), axis=0, tiled=True),
        lax.all_gather(out_weight, ("batch", "ctx"), axis=0, tiled=True),
        lax.all_gather(qkv_bias, ("batch", "ctx"), axis=0, tiled=True),
        lax.all_gather(ln1_gain, ("batch", "ctx"), axis=0, tiled=True),
        lax.all_gather(ln1_shift, ("batch", "ctx"), axis=0, tiled=True),
    )
    branch_two = cotangent.astype(jnp.bfloat16)
    hidden_grad = jnp.dot(branch_two, mlp_back[2], preferred_element_type=jnp.float32)
    unused_value, act_pull = jax.vjp(swish_product, gate_value, up_value)
    gate_grad, up_grad = act_pull(hidden_grad)
    gate_low = gate_grad.astype(jnp.bfloat16)
    up_low = up_grad.astype(jnp.bfloat16)
    normed_two_grad = project_back(gate_low, mlp_back[0]) + project_back(up_low, mlp_back[1])
    unused_two, norm_pull_two = jax.vjp(layer_norm, middle, gain_two, shift_two)
    middle_part, gain_two_grad, shift_two_grad = norm_pull_two(normed_two_grad)
    middle_grad = cotangent + middle_part
    mlp_grads = lax.psum_scatter(
        jnp.concatenate(
            [
                outer_rows(normed_two_low, gate_low),
                outer_rows(normed_two_low, up_low),
                outer_rows(branch_two, hidden_low),
            ],
            axis=1,
        ),
        ("batch", "ctx"),
        scatter_dimension=0,
        tiled=True,
    )
    gate_weight_grad = mlp_grads[:, :FF]
    up_weight_grad = mlp_grads[:, FF : 2 * FF]
    down_weight_grad = mlp_grads[:, 2 * FF :]
    branch_one = middle_grad.astype(jnp.bfloat16)
    out_term = outer_rows(attended_low, branch_one)
    attended_grad = project_back(branch_one, attn_back[1]).astype(jnp.bfloat16)
    grad_heads = attended_grad.reshape(local_rows, H, HD)
    delta = jnp.transpose(
        jnp.sum((attended_grad.astype(jnp.float32) * attended).reshape(local_rows, H, HD), axis=-1)
    )
    key_all, value_all = (
        lax.all_gather(key_rows, "ctx", axis=0, tiled=True),
        lax.all_gather(value_rows, "ctx", axis=0, tiled=True),
    )
    back_rows = 512
    back_count = seq_length // back_rows

    def back_block(query_grad, block):
        key_block, value_block, offset = block
        raw_scores = (
            jnp.einsum("qhd,khd->hqk", queries, key_block, preferred_element_type=jnp.float32)
            * 0.125
        )
        key_places = offset + jnp.arange(back_rows, dtype=jnp.int32)
        allowed = (key_places[None, :] <= places[:, None])[None]
        probs = jnp.where(allowed, jnp.exp(raw_scores - log_total[..., None]), 0.0)
        prob_grad = jnp.einsum(
            "qhd,khd->hqk", grad_heads, value_block, preferred_element_type=jnp.float32
        )
        score_grad = (probs * (prob_grad - delta[..., None])).astype(jnp.bfloat16)
        query_grad = (
            query_grad
            + jnp.einsum("hqk,khd->qhd", score_grad, key_block, preferred_element_type=jnp.float32)
            * 0.125
        )
        key_grad = (
            jnp.einsum("hqk,qhd->khd", score_grad, queries, preferred_element_type=jnp.float32)
            * 0.125
        )
        value_grad = jnp.einsum(
            "hqk,qhd->khd",
            probs.astype(jnp.bfloat16),
            grad_heads,
            preferred_element_type=jnp.float32,
        )
        return (
            query_grad,
            jnp.concatenate(
                [key_grad.reshape(back_rows, D), value_grad.reshape(back_rows, D)], axis=1
            ),
        )

    back_offsets = jnp.arange(back_count, dtype=jnp.int32) * back_rows
    back_blocks = (
        key_all.reshape(back_count, back_rows, H, HD),
        value_all.reshape(back_count, back_rows, H, HD),
        back_offsets,
    )
    query_grad, kv_terms = lax.scan(
        back_block, jnp.zeros((local_rows, H, HD), jnp.float32), back_blocks
    )
    kv_local = lax.psum_scatter(
        kv_terms.reshape(seq_length, 2 * D).astype(jnp.bfloat16),
        "ctx",
        scatter_dimension=0,
        tiled=True,
    ).astype(jnp.float32)

    def turn_heads(heads_in):
        return rotary(heads_in, places)

    unused_three, turn_pull = jax.vjp(turn_heads, pair_heads)
    pair_grad = turn_pull(
        jnp.concatenate([query_grad, kv_local[:, :D].reshape(local_rows, H, HD)], axis=1)
    )[0]
    projected_grad = jnp.concatenate(
        [pair_grad.reshape(local_rows, 2 * D), kv_local[:, D:]], axis=1
    ).astype(jnp.bfloat16)
    qkv_term = outer_rows(normed_low, projected_grad)
    bias_term = jnp.sum(projected_grad.astype(jnp.float32), axis=0)
    normed_grad = project_back(projected_grad, attn_back[0])
    unused_four, norm_pull = jax.vjp(layer_norm, inputs, gain_one, shift_one)
    input_part, gain_one_grad, shift_one_grad = norm_pull(normed_grad)
    tokens_grad = (middle_grad + input_part).reshape(1, local_rows, D)
    summed = (
        lax.psum_scatter(qkv_term, ("batch", "ctx"), scatter_dimension=0, tiled=True),
        lax.psum_scatter(out_term, ("batch", "ctx"), scatter_dimension=0, tiled=True),
        lax.psum_scatter(bias_term, ("batch", "ctx"), scatter_dimension=0, tiled=True),
        lax.psum_scatter(gain_one_grad, ("batch", "ctx"), scatter_dimension=0, tiled=True),
        lax.psum_scatter(shift_one_grad, ("batch", "ctx"), scatter_dimension=0, tiled=True),
        lax.psum_scatter(gain_two_grad, ("batch", "ctx"), scatter_dimension=0, tiled=True),
        lax.psum_scatter(shift_two_grad, ("batch", "ctx"), scatter_dimension=0, tiled=True),
    )
    return (
        mixed.reshape(1, local_rows, D),
        tokens_grad,
        summed[3],
        summed[4],
        summed[0],
        summed[2],
        summed[1],
        summed[5],
        summed[6],
        gate_weight_grad,
        up_weight_grad,
        down_weight_grad,
    )


def solution(mesh):
    in_specs = (
        P("batch", "ctx", None),
        P("batch", "ctx", None),
        P(("batch", "ctx")),
        P(("batch", "ctx")),
        P(("batch", "ctx"), None),
        P(("batch", "ctx")),
        P(("batch", "ctx"), None),
        P(("batch", "ctx")),
        P(("batch", "ctx")),
        P(("batch", "ctx"), None),
        P(("batch", "ctx"), None),
        P(("batch", "ctx"), None),
    )
    out_specs = (
        P("batch", "ctx", None),
        P("batch", "ctx", None),
        P(("batch", "ctx")),
        P(("batch", "ctx")),
        P(("batch", "ctx"), None),
        P(("batch", "ctx")),
        P(("batch", "ctx"), None),
        P(("batch", "ctx")),
        P(("batch", "ctx")),
        P(("batch", "ctx"), None),
        P(("batch", "ctx"), None),
        P(("batch", "ctx"), None),
    )
    return jax.shard_map(local, mesh=mesh, in_specs=in_specs, out_specs=out_specs, check_vma=False)
```

profile of v0, /device:TPU:0, one launch (start us, length us, event | category | flops | bytes accessed | tf_op | source)
XLA Modules:
  0.0 3730.0 jit_solution(5690331719343830301)
XLA Ops:
  7.2 0.7 all-gather.8.cloned.1.call-update
  8.0 0.9 dynamic-update-slice.1
  8.8 0.8 dynamic-update-slice
  9.7 0.8 dynamic-update-slice.4
  10.5 0.8 dynamic-update-slice.3
  11.4 0.8 dynamic-update-slice.2
  12.2 43.6 %all-reduce.15 = (bf16[6144]{0:T(1024)(128)(2,1)S(1)}, bf16[2048]{0:T(1024)(128)(2,1)S(1)}, bf16[2048]{0:T(1024)(128)(2,1)S(1)}, bf16[2048]{0:T(1024)(128)(2,1)S(1)}, bf16[2048]{0:T(1024)(128)(2,1)S(1)}) all-reduce(bf16[6144]{0:T(1024)(128)(2,1)S(1)} %dynamic-update-slice.2, ...), channel_id=1, replica_groups=mesh['batch'=8,'ctx'=4] {'batch','ctx'}, use_global_device_ids=true, to_apply=%add.5 | all-reduce | flops 14336 | bytes 57344
  55.9 1.2 convert_reduce_fusion.1
  57.1 1.3 fusion.35
  58.9 110.8 %all-gather.8.cloned.1.call-done = bf16[2048,6144]{1,0:T(8,128)(2,1)} async-done(((bf16[64,6144]{1,0:T(8,128)(2,1)}), bf16[2048,6144]{1,0:T(8,128)(2,1)}) %all-gather.8.cloned.1.call-update) | async-done | bytes 25165840 | tf_op jit(solution)/shard_map/all_gather | solution.py:74
  169.8 10.3 convolution_add_fusion
  180.1 0.9 slice.65
  181.2 1.5 slice.53
  182.7 1.9 copy.39
  184.9 1.0 maximum_convert_fusion.1
  187.7 0.7 all-gather.20.cloned.1.call-update
  188.6 26.0 all-gather.12.cloned.1.call-done
  214.6 4.0 copy.40
  218.6 33.6 all-gather.10.cloned.1.call-done
  252.2 3.6 select_reduce_fusion
  255.9 2.7 fusion.1
  259.4 2.7 fusion.37
  262.1 1.3 copy.42
  263.4 69.2 %all-gather.14.cloned.1.call-done = bf16[2048,2048]{1,0:T(8,128)(2,1)} async-done(((bf16[64,2048]{1,0:T(8,128)(2,1)}), bf16[2048,2048]{1,0:T(8,128)(2,1)}) %all-gather.14.cloned.1.call-update) | async-done | bytes 8388624 | tf_op jit(solution)/shard_map/all_gather | solution.py:75
  332.6 4.7 fusion.69
  337.9 140.7 %all-gather.16.cloned.1.call-done = bf16[2048,5632]{1,0:T(8,128)(2,1)} async-done(((bf16[64,5632]{1,0:T(8,128)(2,1)}), bf16[2048,5632]{1,0:T(8,128)(2,1)}) %all-gather.16.cloned.1.call-update) | async-done | bytes 23068688 | tf_op jit(solution)/shard_map/all_gather | solution.py:139
  478.5 12.3 fusion.70
  490.8 133.3 %all-gather.18.cloned.1.call-done = bf16[2048,5632]{1,0:T(8,128)(2,1)} async-done(((bf16[64,5632]{1,0:T(8,128)(2,1)}), bf16[2048,5632]{1,0:T(8,128)(2,1)}) %all-gather.18.cloned.1.call-update) | async-done | bytes 23068688 | tf_op jit(solution)/shard_map/all_gather | solution.py:140
  624.1 12.3 fusion.71
  636.4 133.4 %all-gather.20.cloned.1.call-done = bf16[2048,5632]{1,0:T(8,128)(2,1)} async-done(((bf16[64,5632]{1,0:T(8,128)(2,1)}), bf16[2048,5632]{1,0:T(8,128)(2,1)}) %all-gather.20.cloned.1.call-update) | async-done | bytes 23068688 | tf_op jit(solution)/shard_map/all_gather | solution.py:141
  769.8 11.9 multiply_convert_fusion.2
  781.7 18.0 fusion.74
  799.7 12.8 fusion.72
  812.5 14.2 multiply_reduce_fusion
  826.8 1.7 fusion.66
  828.5 0.9 copy-done.12
  829.7 7.5 convert_multiply_fusion
  837.2 1.0 copy.41
  838.2 1.5 copy.43
  839.9 5.5 fusion.14
  845.5 5.4 multiply_convert_fusion
  850.9 0.7 multiply_convert_fusion.1
  851.6 1.3 copy-done.19
  852.9 2.2 pad_maximum_fusion.1
  855.1 6.3 copy.46
  861.6 19.7 convolution_bitcast_fusion
  881.3 18.7 fusion.73
  900.0 88.7 %pad_maximum_fusion = f32[2048,16896]{1,0:T(8,128)} fusion(f32[2048,5632]{1,0:T(8,128)} %convolution_bitcast_fusion, f32[2048,5632]{1,0:T(8,128)} %fusion.74, f32[2048,5632]{1,0:T(8,128)} %fusion.73), kind=kLoop, calls=%fused_computation | loop fusion | flops 69206016 | bytes 276824064 | tf_op jit(solution)/shard_map/concatenate | solution.py:177
  988.8 1.1 copy-done.5
  990.1 8.5 fusion.47
  998.7 1.5 copy-done.23
  1000.2 3.8 fusion.18
  1004.1 1.3 fusion.68
  1007.5 20.7 fusion.44
  1028.2 1.2 copy-done.1
  1029.9 13.2 fusion.13
  1043.6 14.7 fusion.65
  1058.3 1.8 fusion.34
  1060.1 42.5 %all-reduce.14 = (f32[2048]{0:T(1024)S(1)}, f32[2048]{0:T(1024)S(1)}, f32[6144]{0:T(1024)S(1)}, f32[2048]{0:T(1024)S(1)}, f32[2048]{0:T(1024)S(1)}) all-reduce(f32[2048]{0:T(1024)S(1)} %get-tuple-element.58, f32[2048]{0:T(1024)S(1)} %get-tuple-element.61, ...), channel_id=3, replica_groups=mesh['batch'=8,'ctx'=4] {'batch','ctx'}, use_global_device_ids=true, to_apply=%region_13.14.clone | all-reduce | flops 14336 | bytes 114688
  1105.6 2.8 add_bitcast_fusion
  1108.4 1812.1 %all-reduce.18.cloned.1.call-done = f32[2048,16896]{1,0:T(8,128)} async-done(((f32[2048,16896]{1,0:T(8,128)}), f32[2048,16896]{1,0:T(8,128)}) %all-reduce.18.cloned.1.call-update) | async-done | bytes 138412048
  2920.5 5.1 fusion.67
  2925.6 356.4 %reduce-scatter.8.cloned.1.call-done = f32[64,2048]{1,0:T(8,128)} async-done(((f32[2048,2048]{1,0:T(8,128)}), f32[64,2048]{1,0:T(8,128)}) %reduce-scatter.8.cloned.1.call-update) | async-done | bytes 524304 | tf_op jit(solution)/shard_map/reduce_scatter | solution.py:275
  3282.0 441.0 %reduce-scatter.6.cloned.1.call-done = f32[64,6144]{1,0:T(8,128)} async-done(((f32[2048,6144]{1,0:T(8,128)}), f32[64,6144]{1,0:T(8,128)}) %reduce-scatter.6.cloned.1.call-update) | async-done | bytes 1572880 | tf_op jit(solution)/shard_map/reduce_scatter | solution.py:274
  (169 shorter events, 10.9 us)
Async XLA Ops:
  7.2 162.6 %all-gather.8.cloned.1.call-start = ((), (), s32[]{:S(2)}) async-start(), calls=%async_computation.3 | async-start | bytes 25952256 | tf_op jit(solution)/shard_map/all_gather | solution.py:74
  7.9 206.7 %all-gather.12.cloned.1.call-start = ((), (), s32[]{:S(2)}) async-start(), calls=%async_computation.5 | async-start | bytes 2621440 | tf_op jit(solution)/shard_map/all_gather | solution.py:99
  55.8 124.2 %copy-start.33 = (f32[2048]{0:T(1024)}, f32[2048]{0:T(1024)S(1)}, u32[]{:S(2)}) copy-start(f32[2048]{0:T(1024)S(1)} %convert_element_type.90) | copy-start | bytes 24580
  55.8 124.2 %copy-start.26 = (f32[2048]{0:T(1024)}, f32[2048]{0:T(1024)S(1)}, u32[]{:S(2)}) copy-start(f32[2048]{0:T(1024)S(1)} %convert_element_type.89) | copy-start | bytes 24580
  57.1 123.0 %copy-start.41 = (f32[128]{0:T(128)}, f32[128]{0:T(128)S(1)}, u32[]{:S(2)}) copy-start(f32[128]{0:T(128)S(1)} %broadcast_multiply_fusion.1) | copy-start | bytes 1540
  58.9 121.2 %copy-start.45 = (f32[128]{0:T(128)}, f32[128]{0:T(128)S(1)}, u32[]{:S(2)}) copy-start(f32[128]{0:T(128)S(1)} %fusion.51) | copy-start | bytes 1540
  181.0 71.2 %all-gather.10.cloned.1.call-start = ((), (), s32[]{:S(2)}) async-start(), calls=%async_computation.4 | async-start | bytes 2621440 | tf_op jit(solution)/shard_map/all_gather | solution.py:98
  181.2 3.6 copy-start.37
  181.2 3.6 copy-start.39
  184.8 67.5 %copy-start.21 = (bf16[128,64,48]{0,2,1:T(8,128)(2,1)}, bf16[128,64,48]{0,2,1:T(8,128)(2,1)S(1)}, u32[]{:S(2)}) copy-start(bf16[128,64,48]{0,2,1:T(8,128)(2,1)S(1)} %slice.56) | copy-start | bytes 2359300
  184.9 67.4 %copy-start.28 = (bf16[128,64,8]{0,2,1:T(8,128)(2,1)}, bf16[128,64,8]{0,2,1:T(8,128)(2,1)S(1)}, u32[]{:S(2)}) copy-start(bf16[128,64,8]{0,2,1:T(8,128)(2,1)S(1)} %get-tuple-element.93) | copy-start | bytes 393220
  184.9 67.4 %copy-start.30 = (bf16[128,64,8]{0,2,1:T(8,128)(2,1)}, bf16[128,64,8]{0,2,1:T(8,128)(2,1)S(1)}, u32[]{:S(2)}) copy-start(bf16[128,64,8]{0,2,1:T(8,128)(2,1)S(1)} %get-tuple-element.94) | copy-start | bytes 393220
  185.9 146.6 %all-gather.14.cloned.1.call-start = ((), (), s32[]{:S(2)}) async-start(), calls=%async_computation.6 | async-start | bytes 8650752 | tf_op jit(solution)/shard_map/all_gather | solution.py:75
  186.5 292.0 %all-gather.16.cloned.1.call-start = ((), (), s32[]{:S(2)}) async-start(), calls=%async_computation.7 | async-start | bytes 23789568 | tf_op jit(solution)/shard_map/all_gather | solution.py:139
  187.1 437.0 %all-gather.18.cloned.1.call-start = ((), (), s32[]{:S(2)}) async-start(), calls=%async_computation.8 | async-start | bytes 23789568 | tf_op jit(solution)/shard_map/all_gather | solution.py:140
  187.7 582.1 %all-gather.20.cloned.1.call-start = ((), (), s32[]{:S(2)}) async-start(), calls=%async_computation.9 | async-start | bytes 23789568 | tf_op jit(solution)/shard_map/all_gather | solution.py:141
  188.4 815.7 %reduce-scatter.10.cloned.1.call-start = ((), (), s32[]{:S(2)}) async-start(), calls=%async_computation.12 | async-start | bytes 5242880
  188.6 70.7 %copy-start.35 = (pred[128,512]{1,0:T(8,128)(4,1)}, pred[128,512]{1,0:T(8,128)(4,1)S(1)}, u32[]{:S(2)}) copy-start(pred[128,512]{1,0:T(8,128)(4,1)S(1)} %iota_compare_fusion) | copy-start | bytes 196612
  255.8 3.6 copy-start.14
  255.9 3.5 copy-start.24
  259.4 73.2 %copy-start.2 = (bf16[1,128,2048]{2,1,0:T(8,128)(2,1)S(1)}, bf16[1,128,2048]{2,1,0:T(8,128)(2,1)}, u32[]{:S(2)}) copy-start(bf16[1,128,2048]{2,1,0:T(8,128)(2,1)} %param.12) | copy-start | bytes 1572868
  262.1 75.2 %copy-start.4 = (f32[128,32,64]{0,2,1:T(8,128)}, f32[128,32,64]{0,2,1:T(8,128)S(1)}, u32[]{:S(2)}) copy-start(f32[128,32,64]{0,2,1:T(8,128)S(1)} %fusion.37) | copy-start | bytes 3145732
  337.3 489.5 %copy-start = (f32[128,2048]{1,0:T(8,128)}, f32[128,2048]{1,0:T(8,128)S(1)}, u32[]{:S(2)}) copy-start(f32[128,2048]{1,0:T(8,128)S(1)} %get-tuple-element.104) | copy-start | bytes 3145732
  337.6 140.9 %copy-start.50 = (f32[128]{0:T(128)}, f32[128]{0:T(128)S(1)}, u32[]{:S(2)}) copy-start(f32[128]{0:T(128)S(1)} %multiply_reduce_fusion.2) | copy-start | bytes 1540
  490.8 279.0 %copy-start.15 = (bf16[1,128,2048]{2,1,0:T(8,128)(2,1)S(1)}, bf16[1,128,2048]{2,1,0:T(8,128)(2,1)}, u32[]{:S(2)}) copy-start(bf16[1,128,2048]{2,1,0:T(8,128)(2,1)} %param.13) | copy-start | bytes 1572868
  781.7 18.0 copy-start.8
  781.7 79.9 %copy-start.6 = (bf16[128,5632]{1,0:T(8,128)(2,1)}, bf16[128,5632]{1,0:T(8,128)(2,1)S(1)}, u32[]{:S(2)}) copy-start(bf16[128,5632]{1,0:T(8,128)(2,1)S(1)} %get-tuple-element.92) | copy-start | bytes 4325380
  812.5 14.2 copy-start.51
  826.8 2.9 copy-start.20
  828.5 1.0 copy-start.12
  828.5 1.0 copy-start.48
  829.7 7.5 copy-start.17
  837.2 2.7 copy-start.47
  839.9 5.5 copy-start.25
  839.9 5.5 copy-start.32
  839.9 5.5 copy-start.36
  845.4 5.4 copy-start.22
  845.4 5.4 copy-start.29
  845.4 5.4 copy-start.31
  850.9 2.0 copy-start.19
  861.5 2058.9 %all-reduce.18.cloned.1.call-start = ((), (), s32[]{:S(2)}) async-start(), calls=%async_computation.13 | async-start | bytes 276824064
  861.6 19.7 copy-start.9
  988.7 1.2 copy-start.5
  988.7 1.4 copy-start.18
  988.8 2293.2 %reduce-scatter.8.cloned.1.call-start = ((), (), s32[]{:S(2)}) async-start(), calls=%async_computation.11 | async-start | bytes 17301504 | tf_op jit(solution)/shard_map/reduce_scatter | solution.py:275
  998.6 1.6 copy-start.23
  998.7 2724.3 %reduce-scatter.6.cloned.1.call-start = ((), (), s32[]{:S(2)}) async-start(), calls=%async_computation.10 | async-start | bytes 51904512 | tf_op jit(solution)/shard_map/reduce_scatter | solution.py:274
  1005.7 0.7 copy-start.38
  1005.7 0.7 copy-start.40
  1006.4 1.1 copy-start.3
  1006.4 1.0 copy-start.27
  1006.4 1.0 copy-start.34
  1006.4 1.0 copy-start.42
  1006.5 1.0 copy-start.46
  1006.8 21.4 copy-start.10
  1028.2 1.2 copy-start.1
  1028.2 1.7 copy-start.7
  1029.9 13.2 copy-start.11
  1043.6 14.7 copy-start.53
  1043.6 16.5 copy-start.43
  1043.6 16.5 copy-start.44
  1043.6 62.0 %copy-start.13 = (f32[128,2048]{1,0:T(8,128)S(1)}, f32[128,2048]{1,0:T(8,128)}, u32[]{:S(2)}) copy-start(f32[128,2048]{1,0:T(8,128)} %copy-done.12) | copy-start | bytes 3145732
  1043.6 62.0 %copy-start.16 = (bf16[1,128,2048]{2,1,0:T(8,128)(2,1)S(1)}, bf16[1,128,2048]{2,1,0:T(8,128)(2,1)}, u32[]{:S(2)}) copy-start(bf16[1,128,2048]{2,1,0:T(8,128)(2,1)} %param.13) | copy-start | bytes 1572868
  1043.6 62.0 %copy-start.49 = (f32[128]{0:T(128)S(1)}, f32[128]{0:T(128)}, u32[]{:S(2)}) copy-start(f32[128]{0:T(128)} %copy-done.48) | copy-start | bytes 1540
  (1 other events, 0.5 us)
Sparse Core Ops, SparseCore 0:
  10.9 158.8 all-gather.7
  181.1 33.4 all-gather.11
  217.0 35.1 all-gather.9
  255.0 77.5 all-gather.13
  335.3 143.1 all-gather.15
  481.3 142.7 all-gather.17
  627.0 142.7 all-gather.19
  861.6 50.8 reduce-scatter.9
  988.9 1931.5 all-reduce.17
  2923.3 358.6 reduce-scatter.7
  3290.1 432.8 reduce-scatter.5
where the time goes:
time: 3740 us; the launch traced here: 3730 us
  waiting for transfers between devices  3260 us (87%)
  matrix products  221 us (6%)
  other arithmetic  106 us (3%)
  blocking collectives  86.1 us (2%)
  local copies, waits for them, and re-layouts  41.1 us (1%)
    unnamed x13, waiting for transfers between devices  1820 us
    reduce_scatter x1, waiting for transfers between devices, local(): lax.psum_scatter(qkv_term, ('batch', 'ctx'), scatter_dimension=0, tiled=T...  441 us
    reduce_scatter x1, waiting for transfers between devices, local(): lax.psum_scatter(out_term, ('batch', 'ctx'), scatter_dimension=0, tiled=T...  356 us
    all_gather x1, waiting for transfers between devices, local(): lax.all_gather(gate_weight, ('batch', 'ctx'), axis=0, tiled=True)  141 us
    all_gather x1, waiting for transfers between devices, local(): lax.all_gather(down_weight, ('batch', 'ctx'), axis=0, tiled=True)  133 us
    all_gather x1, waiting for transfers between devices, local(): lax.all_gather(up_weight, ('batch', 'ctx'), axis=0, tiled=True)  133 us
    all_gather x1, waiting for transfers between devices, local(): lax.all_gather(qkv_weight, ('batch', 'ctx'), axis=0, tiled=True)  111 us
    concatenate x1, other arithmetic, local(): jnp.concatenate([outer_rows(normed_two_low, gate_low), outer_rows(normed_...  88.7 us
  transfers between devices with their start and end apart: 11, of which 10 were waited for; matrix products, arithmetic and copies ran while one was open for 7% of the time, Pallas kernels for 0%

commit v1 on v0

--- a/solution.py
+++ b/solution.py
@@ -1,6 +1,11 @@
+import functools
+
 import jax
 import jax.numpy as jnp
+import numpy as np
 from jax import lax
+from jax.experimental import pallas as pl
+from jax.experimental.pallas import tpu as pltpu
 from jax.sharding import PartitionSpec as P
 
 D = 2048
@@ -173,22 +178,12 @@
     unused_two, norm_pull_two = jax.vjp(layer_norm, middle, gain_two, shift_two)
     middle_part, gain_two_grad, shift_two_grad = norm_pull_two(normed_two_grad)
     middle_grad = cotangent + middle_part
-    mlp_grads = lax.psum_scatter(
-        jnp.concatenate(
-            [
-                outer_rows(normed_two_low, gate_low),
-                outer_rows(normed_two_low, up_low),
-                outer_rows(branch_two, hidden_low),
-            ],
-            axis=1,
-        ),
-        ("batch", "ctx"),
-        scatter_dimension=0,
-        tiled=True,
-    )
-    gate_weight_grad = mlp_grads[:, :FF]
-    up_weight_grad = mlp_grads[:, FF : 2 * FF]
-    down_weight_grad = mlp_grads[:, 2 * FF :]
+    gate_weight_grad, up_weight_grad, down_weight_grad = (
+        lax.psum_scatter(
+            outer_rows(left, right).astype(jnp.bfloat16), ("batch", "ctx"), scatter_dimension=0, tiled=True
+        ).astype(jnp.float32)
+        for left, right in ((normed_two_low, gate_low), (normed_two_low, up_low), (branch_two, hidden_low))
+    )
     branch_one = middle_grad.astype(jnp.bfloat16)
     out_term = outer_rows(attended_low, branch_one)
     attended_grad = project_back(branch_one, attn_back[1]).astype(jnp.bfloat16)
@@ -295,6 +290,857 @@
     )
 
 
+BF = jnp.bfloat16
+F32 = jnp.float32
+MESH = pl.DeviceIdType.MESH
+ANY = pl.ANY
+VM = pltpu.VMEM
+REMOTE_SEMS = 200
+LOCAL_SEMS = 64
+
+
+def nt(left, right):
+    return lax.dot_general(left, right, (((1,), (1,)), ((), ())), preferred_element_type=F32)
+
+
+def tn(left, right):
+    return lax.dot_general(left, right, (((0,), (0,)), ((), ())), preferred_element_type=F32)
+
+
+def nn(left, right):
+    return jnp.dot(left, right, preferred_element_type=F32)
+
+
+def norm_stats(values):
+    centre = jnp.mean(values, axis=-1, keepdims=True)
+    centred = values - centre
+    spread = jnp.mean(centred * centred, axis=-1, keepdims=True)
+    scale = lax.rsqrt(spread + 1e-05)
+    return centred * scale, scale
+
+
+def norm_back(grad, unit, scale, gain):
+    weighted = grad * gain
+    lead = jnp.mean(weighted, axis=-1, keepdims=True)
+    tilt = jnp.mean(weighted * unit, axis=-1, keepdims=True)
+    return scale * (weighted - lead - unit * tilt)
+
+
+def turn_tables(length):
+    half = ROT // 2
+    freq = (np.float32(10000.0) ** (-np.arange(half, dtype=np.float32) * np.float32(2.0) / np.float32(ROT))).astype(np.float32)
+    angles = np.arange(length, dtype=np.float32)[:, None] * freq[None, :]
+    cosine, sine = np.cos(angles), np.sin(angles)
+    tables = np.zeros((3, length, 128), np.float32)
+    tables[0] = 1.0
+    for start in (0, HD):
+        tables[0, :, start : start + half] = cosine
+        tables[0, :, start + half : start + ROT] = cosine
+        tables[1, :, start : start + half] = -sine
+        tables[2, :, start + half : start + ROT] = sine
+    return tables
+
+
+class Names:
+    pass
+
+
+def layer_kernel(dims, names_in, names_out, names_scratch, *refs):
+    R, C, PL, rows, S, shard, QW, FW = dims
+    r = Names()
+    for name, ref in zip(names_in + names_out + names_scratch, refs):
+        setattr(r, name, ref)
+    batch = lax.axis_index("batch")
+    c = lax.axis_index("ctx")
+    z = batch // 2
+    core = lax.rem(batch, 2)
+    q = core * C + c
+    HS = PL // 2 * rows
+    TOK = PL * rows
+    KB = PL * shard
+    GW = 2 * FW
+
+    counter = [0]
+    local_count = [0]
+
+    def slots(count):
+        first = counter[0]
+        counter[0] += count
+        return first
+
+    def mate(i):
+        other = lax.rem(q + i, PL)
+        return (z * 2 + other // C, lax.rem(other, C))
+
+    def row_mate(i):
+        return (batch, lax.rem(c + i, C))
+
+    sibling = (z * 2 + 1 - core, c)
+
+    def plane_dev(t):
+        return (t * 2 + core, c)
+
+    def rcopy(src, dst, send, recv, dev):
+        return pltpu.make_async_remote_copy(
+            src_ref=src, dst_ref=dst, send_sem=r.ss.at[send], recv_sem=r.rs.at[recv], device_id=dev, device_id_type=MESH
+        )
+
+    drains = []
+
+    def lcopy(src, dst):
+        copy = pltpu.make_async_copy(src, dst, r.ls.at[local_count[0]])
+        local_count[0] += 1
+        copy.start()
+        return copy
+
+    barrier = pltpu.get_barrier_semaphore()
+    for i in range(1, PL):
+        pl.semaphore_signal(barrier, inc=1, device_id=mate(i), device_id_type=MESH)
+    for i in range(1, R):
+        pl.semaphore_signal(barrier, inc=1, device_id=plane_dev(lax.rem(z + i, R)), device_id_type=MESH)
+    pl.semaphore_wait(barrier, PL - 1 + R - 1)
+
+    OFFS = (2, -2, 1, -1)
+
+    class ZGather:
+        def __init__(self, whole, height):
+            self.whole, self.height, self.base = whole, height, slots(5)
+
+        def block(self, s):
+            return self.whole.at[pl.ds(pl.multiple_of(s * self.height, 16), self.height)]
+
+        def start(self, src):
+            for k, off in enumerate(OFFS):
+                t = z + off
+
+                @pl.when((t >= 0) & (t < R))
+                def _():
+                    rcopy(src, self.block(z), self.base + k, self.base + z, plane_dev(t)).start()
+
+                def drain(k=k, t=t):
+                    @pl.when((t >= 0) & (t < R))
+                    def _():
+                        rcopy(src, self.block(z), self.base + k, self.base + z, plane_dev(t)).wait_send()
+
+                drains.append(drain)
+
+        def got(self, s):
+            rcopy(self.block(s), self.block(s), self.base, self.base + s, sibling).wait_recv()
+
+        def relay(self):
+            for at, s, to in ((R - 2, 0, R - 1), (1, R - 1, 0)):
+
+                @pl.when(z == at)
+                def _():
+                    self.got(s)
+                    rcopy(self.block(s), self.block(s), self.base + 4, self.base + s, plane_dev(to)).start()
+
+                def drain(at=at, s=s, to=to):
+                    @pl.when(z == at)
+                    def _():
+                        rcopy(self.block(s), self.block(s), self.base + 4, self.base + s, plane_dev(to)).wait_send()
+
+                drains.append(drain)
+
+        def wait(self):
+            for s in range(R):
+                skip = z == s
+                if s == 0:
+                    skip = skip | (z == R - 2)
+                if s == R - 1:
+                    skip = skip | (z == 1)
+
+                @pl.when(jnp.logical_not(skip))
+                def _():
+                    self.got(s)
+
+    class Spread:
+        def __init__(self, stage):
+            self.stage, self.base = stage, slots(PL)
+
+        def start(self, target):
+            self.target = target
+            for i in range(1, PL):
+                other = lax.rem(q + i, PL)
+                copy = rcopy(self.stage.at[other], target, self.base + i, self.base + i, mate(i))
+                copy.start()
+
+        def wait_send(self):
+            for i in range(1, PL):
+                other = lax.rem(q + i, PL)
+                rcopy(self.stage.at[other], self.target, self.base + i, self.base + i, mate(i)).wait_send()
+
+        def wait(self, block):
+            for i in range(1, PL):
+                rcopy(self.stage.at[0], block(lax.rem(q - i + PL, PL)), self.base + i, self.base + i, mate(i)).wait_recv()
+
+    class Gather:
+        def __init__(self, whole):
+            self.whole, self.base = whole, slots(2 * C)
+
+        def block(self, s):
+            return self.whole.at[pl.ds(pl.multiple_of(s * rows, 16), rows)]
+
+        def start(self, src):
+            self.local = lcopy(src, self.block(q))
+            sends = []
+            for i in range(1, C):
+                sends.append(rcopy(src, self.block(q), self.base + i, self.base + i, row_mate(i)))
+            sends.append(rcopy(src, self.block(q), self.base, self.base, sibling))
+            for copy in sends:
+                copy.start()
+                drains.append(copy.wait_send)
+
+        def relay(self):
+            for i in range(1, C):
+                block = self.block(core * C + lax.rem(c - i + C, C))
+                rcopy(block, block, self.base, self.base + i, sibling).wait_recv()
+                copy = rcopy(block, block, self.base + C - 1 + i, self.base + C - 1 + i, sibling)
+                copy.start()
+                drains.append(copy.wait_send)
+
+        def wait(self):
+            for i in range(C):
+                block = self.block((1 - core) * C + lax.rem(c - i + C, C))
+                sem = self.base if i == 0 else self.base + C - 1 + i
+                rcopy(block, block, self.base, sem, sibling).wait_recv()
+            self.local.wait()
+
+    class Reduce:
+        def __init__(self, k):
+            self.parts, self.from_sib = getattr(r, f"parts{k}"), getattr(r, f"fromsib{k}")
+            self.out, self.got, self.own = getattr(r, f"redout{k}"), getattr(r, f"redin{k}"), getattr(r, f"redown{k}")
+            self.base = slots(C)
+
+        def send_sib(self):
+            copy = rcopy(self.parts.at[0], self.from_sib, self.base, self.base, sibling)
+            copy.start()
+            drains.append(copy.wait_send)
+
+        def middle(self):
+            mine = lcopy(self.parts.at[1], r.mine)
+            rcopy(self.parts.at[0], self.from_sib, self.base, self.base, sibling).wait_recv()
+            theirs = lcopy(self.from_sib, r.theirs)
+            mine.wait()
+            theirs.wait()
+            for i in (1, 2, 3, 0):
+                span = pl.ds(pl.multiple_of(lax.rem(c + i, C) * rows, 16), rows)
+                total = r.mine[span, :].astype(F32) + r.theirs[span, :].astype(F32)
+                if i == 0:
+                    self.own[...] = total
+                else:
+                    self.out[i - 1] = total.astype(BF)
+                    copy = rcopy(self.out.at[i - 1], self.got.at[i - 1], self.base + i, self.base + i, row_mate(i))
+                    copy.start()
+                    drains.append(copy.wait_send)
+
+        def finish(self):
+            for i in range(1, C):
+                rcopy(self.out.at[i - 1], self.got.at[i - 1], self.base + i, self.base + i, row_mate(i)).wait_recv()
+            total = self.own[...]
+            for i in range(1, C):
+                total = total + self.got[i - 1].astype(F32)
+            return total
+
+    middle_plane = (z > 0) & (z < R - 1)
+
+    class ZReduce:
+        def __init__(self, grads, got, extra, relayed, height):
+            self.grads, self.got, self.extra, self.relayed, self.height = grads, got, extra, relayed, height
+            self.base = slots(6)
+
+        def block(self, t):
+            return self.grads.at[pl.ds(pl.multiple_of(t * self.height, 16), self.height)]
+
+        def start(self):
+            for k, off in enumerate(OFFS):
+                t = z + off
+                slot = 2 if abs(off) == 2 else (0 if off == 1 else 1)
+                ok = (t >= 0) & (t < R)
+                if off == 2:
+                    ok = ok & (z != 1)
+                if off == -2:
+                    ok = ok & (z != R - 2)
+
+                def copy(k=k, t=t, slot=slot):
+                    return rcopy(self.block(t), self.got.at[slot], self.base + k, self.base + slot, plane_dev(t))
+
+                @pl.when(ok)
+                def _():
+                    copy().start()
+
+                def drain(ok=ok, copy=copy):
+                    @pl.when(ok)
+                    def _():
+                        copy().wait_send()
+
+                drains.append(drain)
+            for at, owner, via in ((0, R - 1, 1), (R - 1, 0, R - 2)):
+
+                def copy(owner=owner, via=via):
+                    return rcopy(self.block(owner), self.extra, self.base + 4, self.base + 4, plane_dev(via))
+
+                @pl.when(z == at)
+                def _():
+                    copy().start()
+
+                def drain(at=at, copy=copy):
+                    @pl.when(z == at)
+                    def _():
+                        copy().wait_send()
+
+                drains.append(drain)
+
+        def relay(self):
+            @pl.when(middle_plane)
+            def _():
+                owner = jnp.where(z == 1, R - 1, 0)
+                rcopy(self.extra, self.extra, self.base + 4, self.base + 4, sibling).wait_recv()
+
+                def body(a, b, o):
+                    o[...] = (a[...].astype(F32) + b[...].astype(F32)).astype(BF)
+
+                width = self.grads.shape[1]
+                spec = pl.BlockSpec((64, width), lambda i: (i, 0))
+                pltpu.emit_pipeline(body, grid=(self.height // 64,), in_specs=[spec, spec], out_specs=[spec])(
+                    self.block(owner), self.extra, self.relayed
+                )
+                rcopy(self.relayed, self.got.at[2], self.base + 5, self.base + 2, plane_dev(owner)).start()
+
+            def drain():
+                @pl.when(middle_plane)
+                def _():
+                    owner = jnp.where(z == 1, R - 1, 0)
+                    rcopy(self.relayed, self.got.at[2], self.base + 5, self.base + 2, plane_dev(owner)).wait_send()
+
+            drains.append(drain)
+
+        def finish(self, put):
+            @pl.when(z > 0)
+            def _():
+                rcopy(self.got.at[0], self.got.at[0], self.base, self.base, sibling).wait_recv()
+
+            @pl.when(z < R - 1)
+            def _():
+                rcopy(self.got.at[1], self.got.at[1], self.base, self.base + 1, sibling).wait_recv()
+
+            rcopy(self.got.at[2], self.got.at[2], self.base, self.base + 2, sibling).wait_recv()
+            first = jnp.where(z == 0, 1, 0)
+            second = jnp.where(middle_plane, 1, 2)
+
+            def body(own, a, b, d, o):
+                total = own[...].astype(F32) + a[...].astype(F32) + b[...].astype(F32)
+                put(o, total + jnp.where(middle_plane, d[...].astype(F32), 0.0))
+
+            return body, (self.block(z), self.got.at[first], self.got.at[2], self.got.at[second])
+
+    zg_o, zg_qkv = ZGather(r.w_o, shard), ZGather(r.w_qkv, KB)
+    zg_gu, zg_d = ZGather(r.w_gu, KB), ZGather(r.w_d, KB)
+    sp_qkv, sp_gu, sp_d = Spread(r.st_qkv), Spread(r.st_gu), Spread(r.st_d)
+    ag_normed, ag_cot, ag_two, ag_one = Gather(r.a_normed), Gather(r.a_cot), Gather(r.a_two), Gather(r.a_one)
+
+    def mine_rows(whole, height):
+        return whole.at[pl.ds(pl.multiple_of((z * PL + q) * height, 16), height)]
+
+    zg_o.start(r.in_o)
+    local_o = lcopy(r.in_o, zg_o.block(z))
+    base_small = slots(PL)
+    for i in range(1, PL):
+        copy = rcopy(r.in_small, r.small.at[z * PL + q], base_small + i, base_small + i, mate(i))
+        copy.start()
+        drains.append(copy.wait_send)
+    local_small = lcopy(r.in_small, r.small.at[z * PL + q])
+    for other in range(PL):
+        for j in range(3):
+            for zh in range(R):
+                at = j * D + zh * PL * HD + other * HD
+                r.st_qkv[other, :, j * QW + zh * HD : j * QW + (zh + 1) * HD] = r.in_qkv[:, at : at + HD]
+    sp_qkv.start(mine_rows(r.w_qkv, shard))
+    local_qkv = lcopy(r.st_qkv.at[q], mine_rows(r.w_qkv, shard))
+
+    local_small.wait()
+    for i in range(1, PL):
+        rcopy(r.in_small, r.small.at[z * PL + lax.rem(q - i + PL, PL)], base_small, base_small + i, mate(i)).wait_recv()
+    base_smallz = slots(R)
+    plane_small = r.small.at[pl.ds(z * PL, PL)]
+    for i in range(1, R):
+        copy = rcopy(plane_small, plane_small, base_smallz + i, base_smallz + i, plane_dev(lax.rem(z + i, R)))
+        copy.start()
+        drains.append(copy.wait_send)
+    tokens = r.in_tokens[...].astype(F32)
+    unit, _ = norm_stats(tokens)
+    for i in range(1, R):
+        block = r.small.at[pl.ds(lax.rem(z - i + R, R) * PL, PL)]
+        rcopy(block, block, base_smallz, base_smallz + i, sibling).wait_recv()
+    for d in range(R * PL):
+        for k in range(4):
+            r.vec[k : k + 1, shard * d : shard * (d + 1)] = r.small[d, k : k + 1, 0:shard]
+        for k in range(3):
+            r.biases[3 * d + k : 3 * d + k + 1, 0:HD] = r.small[d, 4 + k : 5 + k, 0:HD]
+    for j in range(3):
+        for zh in range(R):
+            row = r.biases[pl.ds(j * H + zh * PL + q, 1), 0:HD]
+            r.bias[0:1, j * QW + zh * HD : j * QW + (zh + 1) * HD] = row
+    r.x_normed[...] = (unit * r.vec[0:1, :] + r.vec[1:2, :]).astype(BF)
+    ag_normed.start(r.x_normed)
+
+    for other in range(PL):
+        at = other * FW
+        r.st_gu[other, :, 0:FW] = r.in_gate[:, at : at + FW]
+        r.st_gu[other, :, FW:GW] = r.in_up[:, at : at + FW]
+        r.st_d[other] = r.in_down[:, at : at + FW]
+
+    local_qkv.wait()
+    sp_qkv.wait(lambda s: r.w_qkv.at[pl.ds(pl.multiple_of((z * PL + s) * shard, 16), shard)])
+    zg_qkv.start(zg_qkv.block(z))
+    sp_gu.start(mine_rows(r.w_gu, shard))
+    local_gu = lcopy(r.st_gu.at[q], mine_rows(r.w_gu, shard))
+    ag_cot.start(r.in_cot)
+    sp_d.start(mine_rows(r.w_d, shard))
+    local_d = lcopy(r.st_d.at[q], mine_rows(r.w_d, shard))
+    zg_o.relay()
+    ag_normed.relay()
+    local_gu.wait()
+    sp_gu.wait(lambda s: r.w_gu.at[pl.ds(pl.multiple_of((z * PL + s) * shard, 16), shard)])
+    zg_gu.start(zg_gu.block(z))
+    zg_qkv.relay()
+    ag_cot.relay()
+    local_d.wait()
+    sp_d.wait(lambda s: r.w_d.at[pl.ds(pl.multiple_of((z * PL + s) * shard, 16), shard)])
+    zg_d.start(zg_d.block(z))
+    ag_normed.wait()
+    zg_qkv.wait()
+
+    TM = HS // 2
+    table_specs = [pl.BlockSpec((TM, 128), lambda i: (lax.rem(i, 2), 0))] * 3
+    tables = [r.tables.at[k] for k in range(3)]
+
+    def qkv_body(x, w, cos, s_one, s_two, o):
+        projected = nn(x[...], w[...]) + r.bias[0:1, :]
+        for piece in range(2 * QW // 128):
+            part = projected[:, piece * 128 : (piece + 1) * 128]
+            turned = part * cos[...] + pltpu.roll(part, 128 - ROT // 2, 1) * s_one[...] + pltpu.roll(part, ROT // 2, 1) * s_two[...]
+            o[:, piece * 128 : (piece + 1) * 128] = turned.astype(BF)
+        o[:, 2 * QW :] = projected[:, 2 * QW :].astype(BF)
+
+    pltpu.emit_pipeline(
+        qkv_body,
+        grid=(TOK // TM,),
+        in_specs=[pl.BlockSpec((TM, D), lambda i: (i, 0)), pl.BlockSpec((D, 3 * QW), lambda i: (0, 0))] + table_specs,
+        out_specs=[pl.BlockSpec((TM, 3 * QW), lambda i: (i, 0))],
+    )(r.a_normed, r.w_qkv, *tables, r.qkv)
+
+    heads = QW // HD
+
+    def softmax_block(queries, keys, first):
+        scores = nt(queries, keys) * 0.125
+        at_query = lax.broadcasted_iota(jnp.int32, scores.shape, 0) + first
+        at_key = lax.broadcasted_iota(jnp.int32, scores.shape, 1)
+        allowed = at_key <= at_query
+        scores = jnp.where(allowed, scores, -1e30)
+        largest = jnp.max(scores, axis=1, keepdims=True)
+        weights = jnp.where(allowed, jnp.exp(scores - largest), 0.0)
+        return weights / jnp.sum(weights, axis=1, keepdims=True)
+
+    QB = HS // 2
+
+    def attention_body(x, o):
+        for h in range(heads):
+            at = h * HD
+            for blk in range(HS // QB):
+                here, seen = blk * QB, (blk + 1) * QB
+                probs = softmax_block(x[here : here + QB, at : at + HD], x[0:seen, QW + at : QW + at + HD], here)
+                out = nn(probs.astype(BF), x[0:seen, 2 * QW + at : 2 * QW + at + HD])
+                o[here : here + QB, at : at + HD] = out.astype(BF)
+
+    pltpu.emit_pipeline(
+        attention_body,
+        grid=(TOK // HS,),
+        in_specs=[pl.BlockSpec((HS, 3 * QW), lambda i: (i, 0))],
+        out_specs=[pl.BlockSpec((HS, QW), lambda i: (i, 0))],
+    )(r.qkv, r.att)
+
+    local_o.wait()
+    zg_o.wait()
+    zg_gu.relay()
+
+    def halves(reduce, source, weight, width, compute):
+        for half in range(2):
+            seq = 1 - core if half == 0 else core
+            part = source.at[pl.ds(pl.multiple_of(seq * HS, 16), HS)]
+
+            def body(x, w, o):
+                o[...] = compute(x[...], w[...]).astype(BF)
+
+            pltpu.emit_pipeline(
+                body,
+                grid=(HS // TM,),
+                in_specs=[pl.BlockSpec((TM, width), lambda i: (i, 0)), pl.BlockSpec(weight.shape, lambda i: (0, 0))],
+                out_specs=[pl.BlockSpec((TM, D), lambda i: (i, 0))],
+            )(part, weight, reduce.parts.at[half])
+            if half == 0:
+                reduce.send_sib()
+
+    red_att = Reduce(0)
+    halves(red_att, r.att, r.w_o, QW, nn)
+    red_att.middle()
+    zg_d.relay()
+    ag_cot.wait()
+    middle = r.in_tokens[...].astype(F32) + red_att.finish()
+    r.middle[...] = middle
+    unit, _ = norm_stats(middle)
+    r.x_two[...] = (unit * r.vec[2:3, :] + r.vec[3:4, :]).astype(BF)
+    ag_two.start(r.x_two)
+    ag_two.relay()
+    ag_two.wait()
+    zg_gu.wait()
+
+    def gu_body(x, w, hid, coef):
+        both = nn(x[...], w[...])
+        gate = both[:, :FW]
+        up = both[:, FW:]
+        sig = 1.0 / (1.0 + jnp.exp(-gate))
+        swish = gate * sig
+        hid[...] = (swish * up).astype(BF)
+        coef[:, :FW] = (up * sig * (1.0 + gate * (1.0 - sig))).astype(BF)
+        coef[:, FW:] = swish.astype(BF)
+
+    pltpu.emit_pipeline(
+        gu_body,
+        grid=(TOK // TM,),
+        in_specs=[pl.BlockSpec((TM, D), lambda i: (i, 0)), pl.BlockSpec((D, GW), lambda i: (0, 0))],
+        out_specs=[pl.BlockSpec((TM, FW), lambda i: (i, 0)), pl.BlockSpec((TM, GW), lambda i: (i, 0))],
+    )(r.a_two, r.w_gu, r.hid, r.coef)
+
+    def weight_grad(acts, grads, out, width, tile):
+        def body(x, g, o):
+            o[...] = tn(x[...], g[...]).astype(BF)
+
+        pltpu.emit_pipeline(
+            body,
+            grid=(acts.shape[1] // tile,),
+            in_specs=[pl.BlockSpec((TOK, tile), lambda i: (0, i)), pl.BlockSpec((TOK, width), lambda i: (0, 0))],
+            out_specs=[pl.BlockSpec((tile, width), lambda i: (i, 0))],
+        )(acts, grads, out)
+
+    zr_d = ZReduce(r.g_d, r.zin_d, r.zx_d, r.zs_d, KB)
+    zr_gu = ZReduce(r.g_gu, r.zin_gu, r.zx_gu, r.zs_gu, KB)
+    zr_o = ZReduce(r.g_o, r.zin_o, r.zx_o, r.zs_o, shard)
+    zr_qkv = ZReduce(r.g_qkv, r.zin_qkv, r.zx_qkv, r.zs_qkv, KB)
+
+    weight_grad(r.a_cot, r.hid, r.g_d, FW, 256)
+    zr_d.start()
+    zg_d.wait()
+
+    def act_back_body(x, w, coef, o):
+        hidden_grad = nn(x[...], w[...])
+        o[:, :FW] = (hidden_grad * coef[:, :FW].astype(F32)).astype(BF)
+        o[:, FW:] = (hidden_grad * coef[:, FW:].astype(F32)).astype(BF)
+
+    pltpu.emit_pipeline(
+        act_back_body,
+        grid=(TOK // TM,),
+        in_specs=[
+            pl.BlockSpec((TM, D), lambda i: (i, 0)),
+            pl.BlockSpec((D, FW), lambda i: (0, 0)),
+            pl.BlockSpec((TM, GW), lambda i: (i, 0)),
+        ],
+        out_specs=[pl.BlockSpec((TM, GW), lambda i: (i, 0))],
+    )(r.a_cot, r.w_d, r.coef, r.gug)
+
+    red_two = Reduce(1)
+    halves(red_two, r.gug, r.w_gu, GW, nt)
+    red_two.middle()
+    weight_grad(r.a_two, r.gug, r.g_gu, GW, 256)
+    zr_gu.start()
+    two_grad = red_two.finish()
+    unit, scale = norm_stats(r.middle[...])
+    middle_grad = r.in_cot[...].astype(F32) + norm_back(two_grad, unit, scale, r.vec[2:3, :])
+    r.middle_grad[...] = middle_grad
+    r.x_one[...] = middle_grad.astype(BF)
+    ag_one.start(r.x_one)
+    r.vec[6:7, :] = jnp.sum(two_grad * unit, axis=0, keepdims=True)
+    r.vec[7:8, :] = jnp.sum(two_grad, axis=0, keepdims=True)
+    red_mixed = Reduce(2)
+    halves(red_mixed, r.hid, r.w_d, FW, nt)
+    ag_one.relay()
+    ag_one.wait()
+
+    def att_grad_body(x, w, o):
+        o[...] = nt(x[...], w[...]).astype(BF)
+
+    pltpu.emit_pipeline(
+        att_grad_body,
+        grid=(TOK // TM,),
+        in_specs=[pl.BlockSpec((TM, D), lambda i: (i, 0)), pl.BlockSpec((QW, D), lambda i: (0, 0))],
+        out_specs=[pl.BlockSpec((TM, QW), lambda i: (i, 0))],
+    )(r.a_one, r.w_o, r.attg)
+
+    def o_grad_body(x, g, o):
+        o[...] = tn(x[...], g[...]).astype(BF)
+
+    pltpu.emit_pipeline(
+        o_grad_body,
+        grid=(D // 512,),
+        in_specs=[pl.BlockSpec((TOK, QW), lambda i: (0, 0)), pl.BlockSpec((TOK, 512), lambda i: (0, i))],
+        out_specs=[pl.BlockSpec((QW, 512), lambda i: (0, i))],
+    )(r.att, r.a_one, r.g_o)
+    zr_o.start()
+    red_mixed.middle()
+    zr_d.relay()
+
+    def attention_back_body(x, g, cos, s_one, s_two, o):
+        for h in range(heads):
+            at = h * HD
+            key_grad = [jnp.zeros((QB, HD), F32) for _ in range(HS // QB)]
+            value_grad = [jnp.zeros((QB, HD), F32) for _ in range(HS // QB)]
+            for blk in range(HS // QB):
+                here, seen = blk * QB, (blk + 1) * QB
+                queries = x[here : here + QB, at : at + HD]
+                keys = x[0:seen, QW + at : QW + at + HD]
+                values = x[0:seen, 2 * QW + at : 2 * QW + at + HD]
+                grads = g[here : here + QB, at : at + HD]
+                probs = softmax_block(queries, keys, here)
+                prob_grad = nt(grads, values)
+                delta = jnp.sum(probs * prob_grad, axis=1, keepdims=True)
+                score_grad = (probs * (prob_grad - delta)).astype(BF)
+                low_probs = probs.astype(BF)
+                r.turn[here : here + QB, at : at + HD] = nn(score_grad, keys) * 0.125
+                key_part = tn(score_grad, queries) * 0.125
+                value_part = tn(low_probs, grads)
+                for k in range(blk + 1):
+                    key_grad[k] = key_grad[k] + key_part[k * QB : (k + 1) * QB]
+                    value_grad[k] = value_grad[k] + value_part[k * QB : (k + 1) * QB]
+            for k in range(HS // QB):
+                r.turn[k * QB : (k + 1) * QB, QW + at : QW + at + HD] = key_grad[k]
+                o[k * QB : (k + 1) * QB, 2 * QW + at : 2 * QW + at + HD] = value_grad[k].astype(BF)
+        for piece in range(2 * QW // 128):
+            part = r.turn[:, piece * 128 : (piece + 1) * 128]
+            back = part * cos[...] + pltpu.roll(part * s_one[...], ROT // 2, 1) + pltpu.roll(part * s_two[...], 128 - ROT // 2, 1)
+            o[:, piece * 128 : (piece + 1) * 128] = back.astype(BF)
+
+    pltpu.emit_pipeline(
+        attention_back_body,
+        grid=(TOK // HS,),
+        in_specs=[pl.BlockSpec((HS, 3 * QW), lambda i: (i, 0)), pl.BlockSpec((HS, QW), lambda i: (i, 0))]
+        + [pl.BlockSpec((HS, 128), lambda i: (0, 0))] * 3,
+        out_specs=[pl.BlockSpec((HS, 3 * QW), lambda i: (i, 0))],
+    )(r.qkv, r.attg, *tables, r.pg)
+
+    weight_grad(r.a_normed, r.pg, r.g_qkv, 3 * QW, 256)
+    zr_qkv.start()
+    red_one = Reduce(3)
+    halves(red_one, r.pg, r.w_qkv, 3 * QW, nt)
+    red_one.middle()
+    zr_gu.relay()
+
+    r.bias[0:1, :] = jnp.zeros((1, 3 * QW), F32)
+
+    def bias_body(x):
+        r.bias[0:1, :] += jnp.sum(x[...].astype(F32), axis=0, keepdims=True)
+
+    pltpu.emit_pipeline(bias_body, grid=(TOK // TM,), in_specs=[pl.BlockSpec((TM, 3 * QW), lambda i: (i, 0))])(r.pg)
+
+    back_d, back_gu, back_qkv = Spread(r.st_d), Spread(r.st_gu), Spread(r.st_qkv)
+
+    def z_sum(reduce, sent, stage, spread, got, width, hbm):
+        sent.wait_send()
+
+        def put(o, total):
+            o[...] = total.astype(BF)
+
+        body, sources = reduce.finish(put)
+        spec = pl.BlockSpec((shard, width), lambda i: (i, 0))
+        pltpu.emit_pipeline(body, grid=(PL,), in_specs=[spec] * 4, out_specs=[spec])(*sources, hbm)
+        load = [lcopy(hbm.at[pl.ds(k * shard, shard)], stage.at[k]) for k in range(PL)]
+        for copy in load:
+            copy.wait()
+        spread.start(got.at[q])
+        return lcopy(stage.at[q], got.at[q])
+
+    local_d = z_sum(zr_d, sp_d, r.st_d, back_d, r.pin_d, FW, r.gp_d)
+    zr_o.relay()
+
+    mixed = r.middle[...] + red_mixed.finish()
+    r.out_mixed[...] = mixed.astype(BF)
+
+    one_grad = red_one.finish()
+    unit, scale = norm_stats(r.in_tokens[...].astype(F32))
+    r.out_tokens[...] = r.middle_grad[...] + norm_back(one_grad, unit, scale, r.vec[0:1, :])
+    r.vec[4:5, :] = jnp.sum(one_grad * unit, axis=0, keepdims=True)
+    r.vec[5:6, :] = jnp.sum(one_grad, axis=0, keepdims=True)
+    r.sg[...] = jnp.zeros_like(r.sg)
+    for d in range(R * PL):
+        for k in range(4):
+            r.sg[d, k : k + 1, 0:shard] = r.vec[4 + k : 5 + k, shard * d : shard * (d + 1)]
+    for j in range(3):
+        for zh in range(R):
+            g = j * H + zh * PL + q
+            r.sg[g // 3, pl.ds(4 + lax.rem(g, 3), 1), 0:HD] = r.bias[0:1, j * QW + zh * HD : j * QW + (zh + 1) * HD]
+    base_sgz = slots(R)
+    for i in range(1, R):
+        t = lax.rem(z + i, R)
+        copy = rcopy(r.sg.at[pl.ds(t * PL, PL)], r.sgz.at[i - 1], base_sgz + i, base_sgz + i, plane_dev(t))
+        copy.start()
+        drains.append(copy.wait_send)
+
+    zr_qkv.relay()
+    local_gu = z_sum(zr_gu, sp_gu, r.st_gu, back_gu, r.pin_gu, GW, r.gp_gu)
+
+    def put_out(o, total):
+        o[...] = total
+
+    body, sources = zr_o.finish(put_out)
+    spec = pl.BlockSpec((shard, 512), lambda i: (0, i))
+    pltpu.emit_pipeline(body, grid=(D // 512,), in_specs=[spec] * 4, out_specs=[spec])(*sources, r.out_o)
+
+    for i in range(1, R):
+        rcopy(r.sgz.at[i - 1], r.sgz.at[i - 1], base_sgz, base_sgz + i, sibling).wait_recv()
+    r.sgs[...] = r.sg[pl.ds(z * PL, PL)] + r.sgz[0] + r.sgz[1] + r.sgz[2]
+    base_sgp = slots(PL)
+    for i in range(1, PL):
+        other = lax.rem(q + i, PL)
+        copy = rcopy(r.sgs.at[other], r.sgp.at[i - 1], base_sgp + i, base_sgp + i, mate(i))
+        copy.start()
+        drains.append(copy.wait_send)
+
+    def pin_block(got):
+        return lambda s: got.at[s]
+
+    local_d.wait()
+    back_d.wait(pin_block(r.pin_d))
+    for other in range(PL):
+        r.out_down[:, other * FW : (other + 1) * FW] = r.pin_d[other].astype(F32)
+
+    local_qkv = z_sum(zr_qkv, sp_qkv, r.st_qkv, back_qkv, r.pin_qkv, 3 * QW, r.gp_qkv)
+    local_gu.wait()
+    back_gu.wait(pin_block(r.pin_gu))
+    for other in range(PL):
+        r.out_gate[:, other * FW : (other + 1) * FW] = r.pin_gu[other, :, 0:FW].astype(F32)
+        r.out_up[:, other * FW : (other + 1) * FW] = r.pin_gu[other, :, FW:GW].astype(F32)
+    total = r.sgs[q]
+    for i in range(1, PL):
+        rcopy(r.sgp.at[i - 1], r.sgp.at[i - 1], base_sgp, base_sgp + i, sibling).wait_recv()
+        total = total + r.sgp[i - 1]
+    r.out_small[...] = total
+    local_qkv.wait()
+    back_qkv.wait(pin_block(r.pin_qkv))
+    for other in range(PL):
+        for j in range(3):
+            for zh in range(R):
+                at = j * D + zh * PL * HD + other * HD
+                r.out_qkv[:, at : at + HD] = r.pin_qkv[other, :, j * QW + zh * HD : j * QW + (zh + 1) * HD].astype(F32)
+    back_d.wait_send()
+    back_gu.wait_send()
+    back_qkv.wait_send()
+    for drain in drains:
+        drain()
+    assert counter[0] <= REMOTE_SEMS and local_count[0] <= LOCAL_SEMS, (counter, local_count)
+
+
+def fast_local(tokens, out_grad, ln1_gain, ln1_shift, qkv_weight, qkv_bias, out_weight, ln2_gain, ln2_shift, gate_weight, up_weight, down_weight):
+    planes, columns = lax.axis_size("batch") // 2, lax.axis_size("ctx")
+    members = 2 * columns
+    rows = tokens.shape[1]
+    seq = rows * columns
+    total = members * rows
+    shard = qkv_weight.shape[0]
+    q_width = D // members
+    f_width = FF // members
+    plane_rows = members * shard
+    dims = (planes, columns, members, rows, seq, shard, q_width, f_width)
+    pieces = jnp.concatenate(
+        [jnp.stack([ln1_gain, ln1_shift, ln2_gain, ln2_shift]), qkv_bias.reshape(3, HD)], axis=0
+    ).astype(F32)
+    small = jnp.pad(pieces, ((0, 1), (0, 128 - HD)))
+    inputs = dict(
+        in_tokens=(tokens.reshape(rows, D), VM),
+        in_cot=(out_grad.reshape(rows, D), VM),
+        in_small=(small, VM),
+        in_qkv=(qkv_weight, VM),
+        in_o=(out_weight, VM),
+        in_gate=(gate_weight, VM),
+        in_up=(up_weight, VM),
+        in_down=(down_weight, VM),
+        tables=(jnp.asarray(turn_tables(seq)), ANY),
+    )
+    outs = dict(
+        out_mixed=((rows, D), BF, VM),
+        out_tokens=((rows, D), F32, VM),
+        out_small=((8, 128), F32, VM),
+        out_qkv=((shard, 3 * D), F32, VM),
+        out_o=((shard, D), F32, ANY),
+        out_gate=((shard, FF), F32, VM),
+        out_up=((shard, FF), F32, VM),
+        out_down=((shard, FF), F32, VM),
+    )
+    final = list(outs)
+    spaces = dict(
+        w_qkv=(D, 3 * q_width), w_o=(q_width, D), w_gu=(D, 2 * f_width), w_d=(D, f_width),
+        a_normed=(total, D), a_cot=(total, D), a_two=(total, D), a_one=(total, D),
+        qkv=(total, 3 * q_width), att=(total, q_width), attg=(total, q_width), pg=(total, 3 * q_width),
+        hid=(total, f_width), coef=(total, 2 * f_width), gug=(total, 2 * f_width),
+        g_qkv=(D, 3 * q_width), g_o=(q_width, D), g_gu=(D, 2 * f_width), g_d=(D, f_width),
+        zin_qkv=(3, plane_rows, 3 * q_width), zin_o=(3, shard, D), zin_gu=(3, plane_rows, 2 * f_width), zin_d=(3, plane_rows, f_width),
+        zx_qkv=(plane_rows, 3 * q_width), zx_o=(shard, D), zx_gu=(plane_rows, 2 * f_width), zx_d=(plane_rows, f_width),
+        zs_qkv=(plane_rows, 3 * q_width), zs_o=(shard, D), zs_gu=(plane_rows, 2 * f_width), zs_d=(plane_rows, f_width),
+        gp_qkv=(plane_rows, 3 * q_width), gp_gu=(plane_rows, 2 * f_width), gp_d=(plane_rows, f_width),
+    )
+    for k in range(4):
+        spaces[f"parts{k}"] = (2, seq, D)
+        spaces[f"fromsib{k}"] = (seq, D)
+    for name, shape in spaces.items():
+        outs[name] = (shape, BF, ANY)
+    scratch = dict(
+        st_qkv=VM((members, shard, 3 * q_width), BF), st_gu=VM((members, shard, 2 * f_width), BF), st_d=VM((members, shard, f_width), BF),
+        pin_qkv=VM((members, shard, 3 * q_width), BF), pin_gu=VM((members, shard, 2 * f_width), BF), pin_d=VM((members, shard, f_width), BF),
+        small=VM((planes * members, 8, 128), F32), sg=VM((planes * members, 8, 128), F32),
+        sgz=VM((3, members, 8, 128), F32), sgs=VM((members, 8, 128), F32), sgp=VM((members - 1, 8, 128), F32),
+        vec=VM((8, D), F32), biases=VM((3 * H, 128), F32), bias=VM((8, 3 * q_width), F32),
+        x_normed=VM((rows, D), BF), x_two=VM((rows, D), BF), x_one=VM((rows, D), BF),
+        middle=VM((rows, D), F32), middle_grad=VM((rows, D), F32),
+        mine=VM((seq, D), BF), theirs=VM((seq, D), BF),
+        turn=VM((seq, 2 * q_width), F32),
+    )
+    for k in range(4):
+        scratch[f"redout{k}"] = VM((columns - 1, rows, D), BF)
+        scratch[f"redin{k}"] = VM((columns - 1, rows, D), BF)
+        scratch[f"redown{k}"] = VM((rows, D), F32)
+    scratch["ss"] = pltpu.SemaphoreType.DMA((REMOTE_SEMS,))
+    scratch["rs"] = pltpu.SemaphoreType.DMA((REMOTE_SEMS,))
+    scratch["ls"] = pltpu.SemaphoreType.DMA((LOCAL_SEMS,))
+    results = pl.pallas_call(
+        functools.partial(layer_kernel, dims, list(inputs), list(outs), list(scratch)),
+        out_shape=[jax.ShapeDtypeStruct(shape, kind) for shape, kind, _ in outs.values()],
+        in_specs=[pl.BlockSpec(memory_space=place) for _, place in inputs.values()],
+        out_specs=[pl.BlockSpec(memory_space=place) for _, _, place in outs.values()],
+        scratch_shapes=list(scratch.values()),
+        compiler_params=pltpu.CompilerParams(collective_id=0, has_side_effects=True, vmem_limit_bytes=62 * 2**20),
+        cost_estimate=pl.CostEstimate(flops=42 * 10**9, bytes_accessed=300 * 10**6, transcendentals=0),
+        name="layer",
+    )(*[array for array, _ in inputs.values()])
+    got = dict(zip(final, results))
+    vectors = got["out_small"][:, :HD]
+    return (
+        got["out_mixed"].reshape(1, rows, D),
+        got["out_tokens"].reshape(1, rows, D),
+        vectors[0],
+        vectors[1],
+        got["out_qkv"],
+        vectors[4:7].reshape(3 * HD),
+        got["out_o"],
+        vectors[2],
+        vectors[3],
+        got["out_gate"],
+        got["out_up"],
+        got["out_down"],
+    )
+
+
+def fits(mesh):
+    return mesh.shape["batch"] == 8 and mesh.shape["ctx"] == 4
+
+
 def solution(mesh):
     in_specs = (
         P("batch", "ctx", None),
@@ -324,4 +1170,5 @@
         P(("batch", "ctx"), None),
         P(("batch", "ctx"), None),
     )
-    return jax.shard_map(local, mesh=mesh, in_specs=in_specs, out_specs=out_specs, check_vma=False)
+    body = fast_local if fits(mesh) else local
+    return jax.shard_map(body, mesh=mesh, in_specs=in_specs, out_specs=out_specs, check_vma=False)

time: 3740 us -> 540 us (0.14)
  waiting for transfers between devices: 3260 us -> 0 us
  Pallas kernels: 0 us -> 521 us
  matrix products: 221 us -> 0 us
  other arithmetic: 106 us -> 0.6 us
  blocking collectives: 86.1 us -> 0 us
    unnamed x13 -> x0, waiting for transfers between devices: 1820 us -> none
    reduce_scatter x2 -> x0, waiting for transfers between devices: 797 us -> none  [the longest x1 441 us: local(): lax.psum_scatter(qkv_term, ('batch', 'ctx'), scatter_dimension=0, tiled=T...]
    all_gather x7 -> x0, waiting for transfers between devices: 647 us -> none  [the longest x1 141 us: local(): lax.all_gather(gate_weight, ('batch', 'ctx'), axis=0, tiled=True)]
    pallas_call x0 -> x1, Pallas kernels: none -> 521 us  [fast_local(): pl.pallas_call(functools.partial(layer_kernel, dims, list(inputs), list(o...]
    dot_general x21 -> x0, matrix products: 221 us -> none  [the longest x5 85.7 us: outer_rows(): lax.dot_general(left, right, (((0,), (0,)), ((), ())), preferred_element_...]
    concatenate x3 -> x0, other arithmetic: 91.1 us -> none  [the longest x1 88.7 us: local(): jnp.concatenate([outer_rows(normed_two_low, gate_low), outer_rows(normed_...]
    unnamed x2 -> x0, blocking collectives: 86.1 us -> none
  transfers between devices with their start and end apart: 11 -> 0, of which waited for: 10 -> 0; matrix products, arithmetic and copies ran while one was open for 7% -> 0% of each run, Pallas kernels for 0% -> 0%
where the time goes in v1:
time: 540 us; the launch traced here: 536 us
  Pallas kernels  521 us (96%)
  local copies, waits for them, and re-layouts  13.7 us (3%)
    pallas_call x1, Pallas kernels, fast_local(): pl.pallas_call(functools.partial(layer_kernel, dims, list(inputs), list(o...  521 us

profile of v1, /device:TPU:0, one launch (start us, length us, event | category | flops | bytes accessed | tf_op | source)
XLA Modules:
  0.0 536.1 jit_solution(15176966032681947715)
XLA Ops:
  0.6 0.7 reshape.44
  1.4 0.7 concatenate.3
  2.1 0.6 pad_convert_fusion.refs_2_
  2.7 521.1 %layer.1 = (bf16[128,2048]{1,0:T(8,128)(2,1)}, f32[128,2048]{1,0:T(8,128)}, f32[8,128]{1,0:T(8,128)}, f32[64,6144]{1,0:T(8,128)}, f32[64,2048]{1,0:T(8,128)}, /*...) custom-call(bf16[128,2048]{1,0:T(8,128)(2,1)} %bitcast.22, ...), custom_call_target="tpu_custom_call" | custom-call | flops 41999998976 | bytes 300000000 | tf_op jit(solution)/shard_map/layer/pallas_call | solution.py:1112
  523.8 0.0 copy-start
  523.8 0.8 slice.23
  524.6 1.3 slice_bitcast_fusion
  525.9 0.6 reshape.47
  526.6 1.9 copy.32
  528.5 0.0 copy-start.4
  528.5 2.4 copy.33
  530.8 0.0 copy-done
  530.8 0.0 copy-start.3
  530.8 1.1 copy.34
  532.0 0.0 copy-done.4
  532.0 0.0 copy-start.2
  532.0 0.8 copy.35
  532.8 0.0 copy-done.3
  532.8 0.0 copy-start.1
  532.8 1.1 copy.36
  533.9 0.0 copy-done.2
  533.9 1.1 copy.37
  535.0 0.0 copy-done.1
  535.0 1.1 copy.38
Async XLA Ops:
  523.8 7.0 %copy-start = (f32[64,6144]{1,0:T(8,128)S(1)}, f32[64,6144]{1,0:T(8,128)}, u32[]{:S(2)}) copy-start(f32[64,6144]{1,0:T(8,128)} %get-tuple-element.48) | copy-start | bytes 4718596
  528.5 3.5 copy-start.4
  530.8 1.9 copy-start.3
  532.0 1.9 copy-start.2
  532.8 2.2 copy-start.1
